TPU v7x, 32 devices: a whole 2x2x4 slice. The times are simulated.
32 devices in a mesh: groups: 2 (over y), pool: 4 (over z), tensor: 2 (over x), rep: 2 (over core).
Axes of the slice: x: 2, y: 2, z: 4, core: 2. Of those that a mesh axis runs over, the one named last changes fastest.
Arguments:
- request_slot: int32 [128], P(('groups', 'pool', 'rep')), parts along dimension 0, may hold values from 0 to 63, as said below
- lengths: int32 [128], P(('groups', 'pool', 'rep')), parts along dimension 0, may hold values from 24 to 192, as said below
- prefill_slot: int32 [16], P(('groups', 'pool', 'rep')), parts along dimension 0, may hold values from 0 to 7
- prefill_offset: int32 [16], P(('groups', 'pool', 'rep')), parts along dimension 0, may hold values from 0 to 184
- queries: bfloat16 [128, 3, 8192], P(('groups', 'pool', 'rep'), None, 'tensor'), parts along dimension 0, may hold values from -8 to 8
- new_kv: bfloat16 [128, 3, 2, 1024], P(('groups', 'pool', 'rep'), None, None, 'tensor'), parts along dimension 0, may hold values from -6 to 6
- kv_cache: bfloat16 [128, 192, 2, 1024], P(('groups', 'pool', 'rep'), None, None, 'tensor'), parts along dimension 0, may hold values from -8 to 8
- prefill_kv: bfloat16 [16, 8, 2, 1024], P('groups', ('pool', 'rep'), None, 'tensor'), parts along dimension 0, may hold values from -6 to 6
- out_weight: bfloat16 [8192, 8192], P('tensor', ('pool', 'rep')), may hold values from -0.5 to 0.5
Outputs:
- layer_out: bfloat16 [384, 8192], P(('groups', 'tensor'), ('pool', 'rep')), parts along dimension 0
There are 2 independent parts, one for each index of `groups`. A program takes and returns all parts, laid end to end along the dimension named above; an argument that names none is the same for every part. Nothing has to cross between parts.
Inputs may be any that keep to these rules, and one draw needn't show every extreme that they name: `request_slot`: A permutation of the 64 slots; slot s lies on pool device s // 8. The 8 requests of one device name at most 2 slots of any one pool device, and in every draw some device names 2 slots of one pool device. Every prefill block lies within its request's length: prefill_offset[o] + 8 <= lengths[o * 8 + prefill_slot[o]].
All inputs are finite; a program needn't handle non-finite values.
Results may differ from a plain program's by a relative error of at most 0.0057.
Values may be sent and summed in bfloat16 or wider, within the bound.
A program may use at most 64 MiB of HBM per device.

v0:
```python
import jax
import jax.numpy as jnp
from jax import lax
from jax.sharding import PartitionSpec as P

HEAD_DIM = 128
DRAFT = 3
CAP = 2


def scores_for(query_slot, key_rows):
    return jnp.einsum(
        "sdkgh,stkh->skgdt", query_slot, key_rows, preferred_element_type=jnp.float32
    ) * HEAD_DIM ** (-0.5)


def attend_whole(query_slot, key_rows, value_rows, fresh_values, slot_lengths, fresh_scores):
    cached_scores = scores_for(query_slot, key_rows)
    visible = jnp.arange(key_rows.shape[1])[None, :] < slot_lengths[:, None]
    cached_scores = jnp.where(visible[:, None, None, None, :], cached_scores, -jnp.inf)
    highest = jnp.maximum(jnp.max(cached_scores, axis=-1), jnp.max(fresh_scores, axis=-1))
    cached_exp = jnp.exp(cached_scores - highest[..., None])
    fresh_exp = jnp.exp(fresh_scores - highest[..., None])
    denominator = jnp.sum(cached_exp, axis=-1) + jnp.sum(fresh_exp, axis=-1)
    cached_weight = (cached_exp / denominator[..., None]).astype(jnp.bfloat16)
    fresh_weight = (fresh_exp / denominator[..., None]).astype(jnp.bfloat16)
    summed = jnp.einsum(
        "skgdt,stkh->sdkgh", cached_weight, value_rows, preferred_element_type=jnp.float32
    )
    return summed + jnp.einsum(
        "skgde,sekh->sdkgh", fresh_weight, fresh_values, preferred_element_type=jnp.float32
    )


def on_device(
    request_slot,
    lengths,
    prefill_slot,
    prefill_offset,
    queries,
    new_kv,
    kv_cache,
    prefill_kv,
    out_weight,
):
    pool_count = lax.axis_size("pool")
    rep_count = lax.axis_size("rep")
    owner_count = pool_count * rep_count
    slot_count = lengths.shape[0]
    kv_width = kv_cache.shape[3]
    query_width = queries.shape[2]
    kv_heads = kv_width // HEAD_DIM
    group_size = query_width // kv_width
    entry_count = owner_count * CAP
    zero_index = jnp.zeros((), jnp.int32)
    pushed = lax.all_to_all(prefill_kv, ("pool", "rep"), split_axis=0, concat_axis=1, tiled=True)
    cache_now = lax.dynamic_update_slice(
        kv_cache, pushed, (prefill_slot[0], prefill_offset[0], zero_index, zero_index)
    )
    owner_of = request_slot // slot_count
    local_of = request_slot % slot_count
    request_ids = jnp.arange(slot_count)
    before = (owner_of[None, :] == owner_of[:, None]) & (
        request_ids[None, :] < request_ids[:, None]
    )
    position = jnp.sum(before.astype(jnp.int32), axis=1)
    target = owner_of * CAP + position
    placing = jnp.arange(entry_count)[:, None] == target[None, :]
    place_matrix = placing.astype(jnp.bfloat16)
    query_pack = (
        jnp.dot(place_matrix, queries.reshape(slot_count, -1), preferred_element_type=jnp.float32)
        .astype(jnp.bfloat16)
        .reshape(owner_count, CAP, DRAFT, query_width)
    )
    pair_pack = (
        jnp.dot(place_matrix, new_kv.reshape(slot_count, -1), preferred_element_type=jnp.float32)
        .astype(jnp.bfloat16)
        .reshape(owner_count, CAP, DRAFT, 2, kv_width)
    )
    slot_pack = jnp.sum(jnp.where(placing, local_of[None, :] + 1, 0), axis=1).reshape(
        owner_count, CAP
    )
    got_query, got_pair, got_slot = (
        lax.all_to_all(query_pack, ("pool", "rep"), split_axis=0, concat_axis=0, tiled=True),
        lax.all_to_all(pair_pack, ("pool", "rep"), split_axis=0, concat_axis=0, tiled=True),
        lax.all_to_all(slot_pack, ("pool", "rep"), split_axis=0, concat_axis=0, tiled=True),
    )
    taking = jnp.arange(slot_count)[:, None] == (got_slot.reshape(entry_count) - 1)[None, :]
    take_matrix = taking.astype(jnp.bfloat16)
    query_slot = (
        jnp.dot(take_matrix, got_query.reshape(entry_count, -1), preferred_element_type=jnp.float32)
        .astype(jnp.bfloat16)
        .reshape(slot_count, DRAFT, kv_heads, group_size, HEAD_DIM)
    )
    fresh_pair = (
        jnp.dot(take_matrix, got_pair.reshape(entry_count, -1), preferred_element_type=jnp.float32)
        .astype(jnp.bfloat16)
        .reshape(slot_count, DRAFT, 2, kv_heads, HEAD_DIM)
    )
    fresh_keys = fresh_pair[:, :, 0]
    fresh_values = fresh_pair[:, :, 1]
    key_rows = cache_now[:, :, 0].reshape(slot_count, -1, kv_heads, HEAD_DIM)
    value_rows = cache_now[:, :, 1].reshape(slot_count, -1, kv_heads, HEAD_DIM)
    causal = jnp.arange(DRAFT)[:, None] >= jnp.arange(DRAFT)[None, :]
    fresh_scores = jnp.einsum(
        "sdkgh,sekh->skgde", query_slot, fresh_keys, preferred_element_type=jnp.float32
    ) * HEAD_DIM ** (-0.5)
    fresh_scores = jnp.where(causal, fresh_scores, -jnp.inf)
    summed = attend_whole(query_slot, key_rows, value_rows, fresh_values, lengths, fresh_scores)
    slot_output = summed.astype(jnp.bfloat16).reshape(slot_count, DRAFT, query_width)
    outgoing = (
        jnp.dot(
            take_matrix.T, slot_output.reshape(slot_count, -1), preferred_element_type=jnp.float32
        )
        .astype(jnp.bfloat16)
        .reshape(owner_count, CAP, DRAFT, query_width)
    )
    returned = lax.all_to_all(outgoing, ("pool", "rep"), split_axis=0, concat_axis=0, tiled=True)
    own_rows = (
        jnp.dot(
            place_matrix.T, returned.reshape(entry_count, -1), preferred_element_type=jnp.float32
        )
        .astype(jnp.bfloat16)
        .reshape(slot_count, DRAFT, query_width)
    )
    gathered = lax.all_gather(own_rows, ("pool", "rep"), axis=0, tiled=True).reshape(
        -1, query_width
    )
    layer_out = lax.psum_scatter(
        jnp.dot(gathered, out_weight, preferred_element_type=jnp.float32),
        "tensor",
        scatter_dimension=0,
        tiled=True,
    )
    return layer_out.astype(jnp.bfloat16)


def solution(mesh):
    return jax.shard_map(
        on_device,
        mesh=mesh,
        in_specs=(
            P(("groups", "pool", "rep")),
            P(("groups", "pool", "rep")),
            P(("groups", "pool", "rep")),
            P(("groups", "pool", "rep")),
            P(("groups", "pool", "rep"), None, "tensor"),
            P(("groups", "pool", "rep"), None, None, "tensor"),
            P(("groups", "pool", "rep"), None, None, "tensor"),
            P("groups", ("pool", "rep"), None, "tensor"),
            P("tensor", ("pool", "rep")),
        ),
        out_specs=P(("groups", "tensor"), ("pool", "rep")),
        check_vma=False,
    )
```

profile of v0, /device:TPU:0, one launch (start us, length us, event | category | flops | bytes accessed | tf_op | source)
XLA Modules:
  0.0 157.7 jit_solution(1427892241727646411)
XLA Ops:
  6.5 0.7 copy-done.6
  8.2 6.6 %all-to-all-start = ((s32[8,1,2]{2,1,0:T(1,128)}), s32[8,1,2]{2,1,0:T(1,128)S(1)}, u32[]{:S(2)}, u32[]{:S(2)}) async-start(s32[8,1,2]{2,1,0:T(1,128)} %bitcast), calls=%async_computation | async-start | bytes 8192 | tf_op jit(solution)/shard_map/all_to_all | solution.py:86
  14.8 1.1 convolution_convert_fusion.1
  15.9 2.3 %reshape.85 = bf16[8,2,3,4096]{3,2,1,0:T(4,128)(2,1)} reshape(bf16[16,12288]{1,0:T(8,128)(2,1)} %convolution_convert_fusion.1) | data formatting | bytes 786432 | tf_op jit(solution)/shard_map/reshape | solution.py:73
  18.3 2.3 %copy.36 = bf16[8,2,3,4096]{3,1,2,0:T(2,128)(2,1)} copy(bf16[8,2,3,4096]{3,2,1,0:T(4,128)(2,1)} %reshape.85) | data formatting | bytes 786432 | tf_op jit(solution)/shard_map/reshape | solution.py:73
  20.9 0.7 reshape.89
  23.0 5.1 %all-to-all-start.1 = ((bf16[8,1,2,512]{3,2,1,0:T(2,128)(2,1)}), bf16[8,1,2,512]{3,2,1,0:T(2,128)(2,1)S(1)}, u32[]{:S(2)}, u32[]{:S(2)}) async-start(bf16[8,1,2,512]{3,2,1,0:T(2,128)(2,1)} %param.16), calls=%async_computation.1 | async-start | bytes 32768 | tf_op jit(solution)/shard_map/all_to_all | solution.py:56
  28.2 5.6 %all-to-all-done.1 = bf16[8,1,2,512]{3,2,1,0:T(2,128)(2,1)S(1)} async-done(((bf16[8,1,2,512]{3,2,1,0:T(2,128)(2,1)}), bf16[8,1,2,512]{3,2,1,0:T(2,128)(2,1)S(1)}, u32[]{:S(2)}, u32[]{:S(2)}) %all-to-all-start.1) | async-done | bytes 16416 | tf_op jit(solution)/shard_map/all_to_all | solution.py:56
  33.7 3.4 %all-to-all-start.3 = ((bf16[8,2,3,2,512]{4,3,2,1,0:T(2,128)(2,1)}), bf16[8,2,3,2,512]{4,3,2,1,0:T(2,128)(2,1)S(1)}, u32[]{:S(2)}, u32[]{:S(2)}) async-start(bf16[8,2,3,2,512]{4,3,2,1,0:T(2,128)(2,1)} %reshape.89), calls=%async_computation.3 | async-start | bytes 196608 | tf_op jit(solution)/shard_map/all_to_all | solution.py:85
  37.1 6.2 %all-to-all-done.3 = bf16[8,2,3,2,512]{4,3,2,1,0:T(2,128)(2,1)S(1)} async-done(((bf16[8,2,3,2,512]{4,3,2,1,0:T(2,128)(2,1)}), bf16[8,2,3,2,512]{4,3,2,1,0:T(2,128)(2,1)S(1)}, u32[]{:S(2)}, u32[]{:S(2)}) %all-to-all-start.3) | async-done | bytes 98336 | tf_op jit(solution)/shard_map/all_to_all | solution.py:85
  43.4 4.1 %all-to-all-start.2 = ((bf16[8,2,3,4096]{3,1,2,0:T(2,128)(2,1)}), bf16[8,2,3,4096]{3,1,2,0:T(2,128)(2,1)}, u32[]{:S(2)}, u32[]{:S(2)}) async-start(bf16[8,2,3,4096]{3,1,2,0:T(2,128)(2,1)} %copy.36), calls=%async_computation.2 | async-start | bytes 786432 | tf_op jit(solution)/shard_map/all_to_all | solution.py:84
  47.5 18.7 %slice_reduce_fusion.1 = (bf16[8,192,512]{2,1,0:T(8,128)(2,1)}, bf16[8,192,512]{2,1,0:T(8,128)(2,1)}) fusion(bf16[8,192,2,512]{3,2,1,0:T(2,128)(2,1)S(1)} %bitcast_dynamic-update-slice_fusion), kind=kLoop, calls=%fused_computation.7 | loop fusion | bytes 6291456 | tf_op jit(solution)/shard_map/slice | solution.py:103
  66.2 3.6 %reshape_squeeze.7 = bf16[8,192,4,128]{3,2,1,0:T(4,128)(2,1)} reshape(bf16[8,192,512]{2,1,0:T(8,128)(2,1)} %get-tuple-element.6) | data formatting | bytes 3145728 | tf_op jit(solution)/shard_map/reshape;squeeze | solution.py:102
  70.5 1.5 copy.37
  72.4 0.8 fusion.45
  73.2 1.0 fusion.44
  77.2 17.3 %all_to_all.36 = bf16[8,2,3,4096]{3,1,2,0:T(2,128)(2,1)S(1)} all-to-all(bf16[8,2,3,4096]{3,1,2,0:T(2,128)(2,1)S(1)} %copy.45), channel_id=1, replica_groups=mesh['groups'=2,'pool'=4,'tensor'=2,'rep'=2] {'pool','rep'}, dimensions={0} | all-to-all | bytes 786432 | tf_op jit(solution)/shard_map/all_to_all | solution.py:118
  95.1 0.9 convolution_convert_fusion.2
  96.3 23.9 %all-gather.2.cloned.1.call-done = bf16[64,3,4096]{2,0,1:T(8,128)(2,1)} async-done(((bf16[8,3,4096]{2,0,1:T(8,128)(2,1)}), bf16[64,3,4096]{2,0,1:T(8,128)(2,1)}) %all-gather.2.cloned.1.call-update) | async-done | bytes 1572880 | tf_op jit(solution)/shard_map/all_gather | solution.py:126
  120.2 2.8 %copy.47 = bf16[64,3,4096]{2,1,0:T(4,128)(2,1)S(1)} copy(bf16[64,3,4096]{2,0,1:T(8,128)(2,1)} %all-gather.2.cloned.1.call-done) | data formatting | bytes 3145728 | tf_op jit(solution)/shard_map/all_gather | solution.py:126
  123.0 2.5 %reshape.95 = bf16[192,4096]{1,0:T(8,128)(2,1)} reshape(bf16[64,3,4096]{2,1,0:T(4,128)(2,1)S(1)} %copy.47) | data formatting | bytes 3145728 | tf_op jit(solution)/shard_map/reshape | solution.py:126
  125.5 6.6 %fusion.46 = f32[192,1024]{1,0:T(8,128)} fusion(bf16[192,4096]{1,0:T(8,128)(2,1)} %reshape.95, bf16[4096,1024]{1,0:T(8,128)(2,1)} %param.17), kind=kOutput, calls=%fused_computation.64 | convolution fusion | flops 1610612736 | bytes 10747904 | tf_op jit(solution)/shard_map/dot_general | solution.py:130
  132.1 17.1 %reduce-scatter.2.cloned.1.call-done = f32[96,1024]{1,0:T(8,128)} async-done(((f32[192,1024]{1,0:T(8,128)}), f32[96,1024]{1,0:T(8,128)}) %reduce-scatter.2.cloned.1.call-update) | async-done | bytes 393232 | tf_op jit(solution)/shard_map/reduce_scatter | solution.py:129
  149.2 1.7 %convert_element_type.49 = bf16[96,1024]{1,0:T(8,128)(2,1)} convert(f32[96,1024]{1,0:T(8,128)} %reduce-scatter.2.cloned.1.call-done) | non-fusion elementwise | flops 98304 | bytes 589824 | tf_op jit(solution)/shard_map/convert_element_type | solution.py:135
  (49 shorter events, 6.4 us)
Async XLA Ops:
  6.5 8.3 %copy-start = (bf16[8,3,4096]{2,0,1:T(8,128)(2,1)S(1)}, bf16[8,3,4096]{2,0,1:T(8,128)(2,1)}, u32[]{:S(2)}) copy-start(bf16[8,3,4096]{2,0,1:T(8,128)(2,1)} %param.13) | copy-start | bytes 589828
  6.5 0.7 copy-start.6
  6.5 14.0 %copy-start.4 = (bf16[8,3,2,512]{3,2,1,0:T(2,128)(2,1)S(1)}, bf16[8,3,2,512]{3,2,1,0:T(2,128)(2,1)}, u32[]{:S(2)}) copy-start(bf16[8,3,2,512]{3,2,1,0:T(2,128)(2,1)} %param.14) | copy-start | bytes 147460
  7.2 15.7 %copy-start.5 = (s32[8]{0:T(128)S(1)}, s32[8]{0:T(128)}, u32[]{:S(2)}) copy-start(s32[8]{0:T(128)} %param.10) | copy-start | bytes 100
  8.2 28.9 %copy-start.1 = (bf16[8,192,2,512]{3,2,1,0:T(2,128)(2,1)S(1)}, bf16[8,192,2,512]{3,2,1,0:T(2,128)(2,1)}, u32[]{:S(2)}) copy-start(bf16[8,192,2,512]{3,2,1,0:T(2,128)(2,1)} %param.15) | copy-start | bytes 9437188
  8.2 14.8 %all-to-all-start = ((s32[8,1,2]{2,1,0:T(1,128)}), s32[8,1,2]{2,1,0:T(1,128)S(1)}, u32[]{:S(2)}, u32[]{:S(2)}) async-start(s32[8,1,2]{2,1,0:T(1,128)} %bitcast), calls=%async_computation | async-start | bytes 8192 | tf_op jit(solution)/shard_map/all_to_all | solution.py:86
  23.0 10.7 %all-to-all-start.1 = ((bf16[8,1,2,512]{3,2,1,0:T(2,128)(2,1)}), bf16[8,1,2,512]{3,2,1,0:T(2,128)(2,1)S(1)}, u32[]{:S(2)}, u32[]{:S(2)}) async-start(bf16[8,1,2,512]{3,2,1,0:T(2,128)(2,1)} %param.16), calls=%async_computation.1 | async-start | bytes 32768 | tf_op jit(solution)/shard_map/all_to_all | solution.py:56
  33.7 9.6 %all-to-all-start.3 = ((bf16[8,2,3,2,512]{4,3,2,1,0:T(2,128)(2,1)}), bf16[8,2,3,2,512]{4,3,2,1,0:T(2,128)(2,1)S(1)}, u32[]{:S(2)}, u32[]{:S(2)}) async-start(bf16[8,2,3,2,512]{4,3,2,1,0:T(2,128)(2,1)} %reshape.89), calls=%async_computation.3 | async-start | bytes 196608 | tf_op jit(solution)/shard_map/all_to_all | solution.py:85
  43.4 27.1 %all-to-all-start.2 = ((bf16[8,2,3,4096]{3,1,2,0:T(2,128)(2,1)}), bf16[8,2,3,4096]{3,1,2,0:T(2,128)(2,1)}, u32[]{:S(2)}, u32[]{:S(2)}) async-start(bf16[8,2,3,4096]{3,1,2,0:T(2,128)(2,1)} %copy.36), calls=%async_computation.2 | async-start | bytes 786432 | tf_op jit(solution)/shard_map/all_to_all | solution.py:84
  47.5 72.7 %all-gather.2.cloned.1.call-start = ((), (), s32[]{:S(2)}) async-start(), calls=%async_computation.6 | async-start | bytes 1769472 | tf_op jit(solution)/shard_map/all_gather | solution.py:126
  66.2 3.6 %copy-start.2 = (bf16[8,192,512]{2,1,0:T(8,128)(2,1)S(1)}, bf16[8,192,512]{2,1,0:T(8,128)(2,1)}, u32[]{:S(2)}) copy-start(bf16[8,192,512]{2,1,0:T(8,128)(2,1)} %get-tuple-element.5) | copy-start | bytes 4718596
  70.4 2.7 %copy-start.3 = (bf16[8,192,4,128]{3,2,1,0:T(4,128)(2,1)S(1)}, bf16[8,192,4,128]{3,2,1,0:T(4,128)(2,1)}, u32[]{:S(2)}) copy-start(bf16[8,192,4,128]{3,2,1,0:T(4,128)(2,1)} %reshape_squeeze.7) | copy-start | bytes 4718596
  96.1 53.1 %reduce-scatter.2.cloned.1.call-start = ((), (), s32[]{:S(2)}) async-start(), calls=%async_computation.7 | async-start | bytes 1179648 | tf_op jit(solution)/shard_map/reduce_scatter | solution.py:129
Sparse Core Ops, SparseCore 0:
  96.2 23.9 all-gather.1
  132.2 16.9 reduce-scatter.1
where the time goes:
time: 158 us
  waiting for transfers between devices  52.8 us (33%)
  local copies, waits for them, and re-layouts  38.3 us (24%)
  starting transfers between devices  19.4 us (12%)
  blocking collectives  17.3 us (11%)
  between operations  14.9 us (9%)
  matrix products  12.2 us (8%)
  other arithmetic  2.7 us (2%)
    all_gather x1, waiting for transfers between devices, on_device(): lax.all_gather(own_rows, ('pool', 'rep'), axis=0, tiled=True)  23.9 us
    slice x1, local copies, waits for them, and re-layouts, on_device(): value_rows = cache_now[:, :, 1].reshape(slot_count, -1, kv_heads, HEAD_DIM)  18.7 us
    all_to_all x1, blocking collectives, on_device(): lax.all_to_all(outgoing, ('pool', 'rep'), split_axis=0, concat_axis=0, ti...  17.3 us
    reduce_scatter x1, waiting for transfers between devices, on_device(): lax.psum_scatter(jnp.dot(gathered, out_weight, preferred_element_type=jnp...  17.1 us
    all_to_all x1, starting transfers between devices, on_device(): lax.all_to_all(slot_pack, ('pool', 'rep'), split_axis=0, concat_axis=0, t...  6.59 us
    dot_general x1, matrix products, on_device(): jnp.dot(gathered, out_weight, preferred_element_type=jnp.float32)  6.55 us
    all_to_all x1, waiting for transfers between devices, on_device(): lax.all_to_all(pair_pack, ('pool', 'rep'), split_axis=0, concat_axis=0, t...  6.23 us
    all_to_all x1, waiting for transfers between devices, on_device(): lax.all_to_all(prefill_kv, ('pool', 'rep'), split_axis=0, concat_axis=1,...  5.55 us
  transfers between devices with their start and end apart: 6, of which 4 were waited for; matrix products, arithmetic and copies ran while one was open for 19% of the time, Pallas kernels for 0%

commit v1 on v0

v1 whole, which is shorter than its diff:
```python
import functools

import jax
import jax.numpy as jnp
from jax import lax
from jax.experimental import pallas as pl
from jax.experimental.pallas import tpu as pltpu
from jax.sharding import PartitionSpec as P

HD = 128
DRAFT = 3
CAP = 2
KEYS = 64
PACK = 64
F32 = jnp.float32
BF16 = jnp.bfloat16
MESH = pl.DeviceIdType.MESH


def log2(n):
    assert n & (n - 1) == 0
    return n.bit_length() - 1


def up(n, m):
    return (n + m - 1) // m * m


def iota(shape, dim):
    return lax.broadcasted_iota(jnp.int32, shape, dim)


def kernel(dims, slot_s, len_s, pslot_s, poff_s, src, cache, weight, out,
           kvbuf, wbuf, pack, recv, meta_out, meta_in, perm, cmat, gath, ytot, ysend, yrecv,
           kv_sem, w_sem, self_sem, pk_send, pk_recv, mt_send, mt_recv, g_send, g_recv, y_send, y_recv):
    S, O, R, T, K, CTX, GS, N, NT = dims
    PL = O // R
    ls, lo = log2(S), log2(O)
    lg = log2(GS)
    gw = GS * HD
    half = GS // 2
    PR = max(16, O)
    z, core, me_t = lax.axis_index("pool"), lax.axis_index("rep"), lax.axis_index("tensor")
    me = z * R + core
    rows_t = S * O * DRAFT // T

    for k in range(K):
        pltpu.make_async_copy(
            cache.at[:, :, :, pl.ds(k * HD, HD)], kvbuf.at[k], kv_sem.at[k]).start()
    for k in range(K):
        pltpu.make_async_copy(
            weight.at[pl.ds(k * gw, gw), :], wbuf.at[k], w_sem.at[k]).start()

    barrier = pltpu.get_barrier_semaphore()
    for i in range(1, O):
        p = lax.rem(me + i, O)
        pl.semaphore_signal(barrier, inc=1, device_id={"pool": p // R, "rep": lax.rem(p, R)},
                            device_id_type=MESH)
    for i in range(1, T):
        pl.semaphore_signal(barrier, inc=1, device_id={"tensor": lax.rem(me_t + i, T)},
                            device_id_type=MESH)

    slots = [slot_s[r] for r in range(S)]
    orow = iota((O, 128), 0)
    lane = iota((O, 128), 1)
    seen = jnp.zeros((O, 128), jnp.int32)
    note = jnp.zeros((O, 128), jnp.int32)
    for r in range(S):
        hit = orow == (slots[r] >> ls)
        note = jnp.where(hit & (seen == (lane & 1)), (slots[r] & (S - 1)) + 1, note)
        seen = seen + jnp.where(hit, 1, 0)
    MR = meta_out.shape[1]
    L = (iota((MR, 128), 0) - 1) * 128 + iota((MR, 128), 1) - me * (S * DRAFT)
    keyed = jnp.zeros((MR, 128), jnp.int32)
    for r in range(S):
        keyed = jnp.where((L >= DRAFT * r) & (L < DRAFT * r + DRAFT),
                          slots[r] * 4 + 1 - DRAFT * r + L, keyed)
    first = iota((MR, 128), 0) == 0
    for o in range(O):
        meta_out[o] = jnp.where(first, jnp.broadcast_to(note[o:o + 1], (MR, 128)), keyed)

    NQ, NF = S * DRAFT * GS, S * DRAFT * 2
    NC = src.shape[0]
    c = iota((1, NC), 1)
    f = c - NQ
    pre = c - NQ - NF
    is_q = c < NQ
    is_f = (c >= NQ) & (pre < 0)
    rcol = jnp.where(is_q, (c >> lg) & (S - 1), jnp.where(is_f, (f >> 1) & (S - 1), -1))
    ocol = jnp.zeros((1, NC), jnp.int32) - 1
    for r in range(S):
        ocol = jnp.where(rcol == r, slots[r] >> ls, ocol)
    rank = jnp.zeros((1, NC), jnp.int32)
    for r in range(S):
        rank = rank + jnp.where((rcol > r) & (ocol == (slots[r] >> ls)), 1, 0)
    code = (ocol * CAP + rank) * KEYS
    ckey = jnp.where(
        is_q, code + (c >> (lg + ls)) * GS + (c & (GS - 1)),
        jnp.where(is_f, code + 24 + (f >> (1 + ls)) * 2 + (f & 1),
                  (pre >> 1) * CAP * KEYS + 32 + (pre & 1)))
    OB = min(O, 8)
    jr = iota((OB * PACK, 1), 0)
    j = jr & (PACK - 1)
    jf = j - 48
    jkey = jnp.where(j < 48, (j & 1) * KEYS + (j >> 4) * GS + ((j >> 1) & (GS - 1)),
                     jnp.where(j < 60, (j & 1) * KEYS + 24 + (jf >> 2) * 2 + ((jf >> 1) & 1),
                               jnp.where(j < 62, 32 + j - 60, -1000000)))
    jkey = jkey + (jr >> 6) * CAP * KEYS
    for b in range(O // OB):
        place = jnp.where(jkey + b * OB * CAP * KEYS == ckey, 1.0, 0.0).astype(BF16)
        packed = jnp.dot(place, src[...], preferred_element_type=F32).astype(BF16)
        for k in range(K):
            pack[k, b * OB:(b + 1) * OB] = packed[:, k * HD:(k + 1) * HD].reshape(OB, PACK, HD)

    pl.semaphore_wait(barrier, O - 1 + T - 1)

    def peer(i):
        p = lax.rem(me + i, O)
        return p, {"pool": p // R, "rep": lax.rem(p, R)}

    def meta_copy(i):
        p, dev = peer(i)
        return pltpu.make_async_remote_copy(
            meta_out.at[p], meta_in.at[me], mt_send.at[p], mt_recv.at[me], dev, MESH)

    def pack_copy(k, i):
        p, dev = peer(i)
        return pltpu.make_async_remote_copy(
            pack.at[k, p], recv.at[k, me], pk_send.at[k, p], pk_recv.at[k, me], dev, MESH)

    own_copies = [pltpu.make_async_copy(meta_out.at[me], meta_in.at[me], self_sem.at[K])]
    for k in range(K):
        own_copies.append(pltpu.make_async_copy(pack.at[k, me], recv.at[k, me], self_sem.at[k]))
    for cp in own_copies:
        cp.start()
    order = list(range(1, O))
    for i in order:
        meta_copy(i).start()
    for k in range(K):
        for i in order:
            pack_copy(k, i).start()

    def wait_arrival(buf, sem):
        pltpu.make_async_copy(buf, buf, sem).wait()

    own_copies[0].wait()
    for i in order:
        p, _ = peer(i)
        wait_arrival(meta_in.at[p], mt_recv.at[p])

    def row_keys():
        q = iota((NQ, 1), 0)
        qk = (((q >> lg) & (S - 1)) + 1) * KEYS + (q >> (lg + ls)) * GS + (q & (GS - 1))
        fr = iota((S * 16, 1), 0)
        e = fr & 15
        pr = iota((PR, 1), 0)
        parts = [qk]
        for kv in range(2):
            parts.append(jnp.where(e < DRAFT, ((fr >> 4) + 1) * KEYS + 24 + e * 2 + kv, -2))
            parts.append(jnp.where(pr < O, (S + 2) * KEYS + pr * 2 + kv, -2))
        return parts

    parts = row_keys()
    l128 = iota((1, 128), 1)
    jl = l128 & (PACK - 1)
    jlf = jl - 48
    stat = jnp.where(jl < 48, (jl >> 4) * GS + ((jl >> 1) & (GS - 1)),
                     24 + (jlf >> 2) * 2 + ((jlf >> 1) & 1))
    for pair in range(O // 2):
        m = jnp.where(l128 < PACK, meta_in[2 * pair, 0:1, :], meta_in[2 * pair + 1, 0:1, :])
        srcidx = 2 * pair + (l128 >> 6)
        key = jnp.where(jl < 60, m * KEYS + stat,
                        jnp.where(jl < 62, (S + 2) * KEYS + srcidx * 2 + jl - 60, -1))
        row = 0
        for part in parts:
            n = part.shape[0]
            perm[row:row + n, pair * 128:(pair + 1) * 128] = jnp.where(part == key, 1.0, 0.0).astype(BF16)
            row += n

    def out_onehots(keys):
        g = iota((O * 2 * S, 1), 0)
        hi = (g >> ls) & 1
        slot4 = (((g >> (ls + 1)) << ls) + (g & (S - 1))) * 4 + 1
        res = []
        for kk in (slot4 + hi, jnp.where(hi == 0, slot4 + 2, -1), jnp.where(hi == 1, slot4 + 2, -1)):
            res.append(jnp.transpose(jnp.where(kk == keys, 1.0, 0.0)).astype(BF16))
        return res

    total = meta_in[0]
    for o in range(1, O):
        total = total + meta_in[o]
    keep = cmat is not None
    if keep:
        for t in range(NT):
            for x, m in enumerate(out_onehots(total[1 + t:2 + t])):
                cmat[x, t * 128:(t + 1) * 128, :] = m
    else:
        for i in order:
            meta_copy(i).wait_send()
        meta_out[0] = total

    pslot, poff = pslot_s[0], poff_s[0]
    jc = iota((1, 2 * CTX), 1)
    tc = jc >> 1
    neg = jnp.float32(-jnp.inf)
    lp = iota((1, PR + 16), 1)
    drow = iota((DRAFT * GS, PR + 16), 0) >> lg
    lane_e = iota((DRAFT * GS, PR + 16), 1)
    fresh_ok = (lane_e >= PR) & (lane_e - PR <= drow)
    scale = HD ** -0.5
    si = iota((S * GS, S * GS), 0)
    sj = iota((S * GS, S * GS), 1)
    swap = jnp.where(((si & (S - 1)) == (sj >> lg)) & ((si >> ls) == (sj & (GS - 1))), 1.0, 0.0).astype(BF16)

    def attend(k):
        took = jnp.dot(perm[...], recv[k].reshape(O * PACK, HD), preferred_element_type=F32)
        fk0 = NQ
        pk0 = fk0 + S * 16
        fv0 = pk0 + PR
        pv0 = fv0 + S * 16
        pre_k, pre_v = took[pk0:pk0 + PR].astype(BF16), took[pv0:pv0 + PR].astype(BF16)
        sc, se, xs, vs = [], [], [], []
        for s in range(S):
            q = jnp.concatenate([took[(d * S + s) * GS:(d * S + s + 1) * GS] for d in range(DRAFT)], 0).astype(BF16)
            x = kvbuf[k, s].reshape(2 * CTX, HD)
            ek = jnp.concatenate([pre_k, took[fk0 + s * 16:fk0 + s * 16 + 16].astype(BF16)], 0)
            ev = jnp.concatenate([pre_v, took[fv0 + s * 16:fv0 + s * 16 + 16].astype(BF16)], 0)
            nt = (((1,), (1,)), ((), ()))
            a = lax.dot_general(q, x, nt, preferred_element_type=F32) * scale
            b = lax.dot_general(q, ek, nt, preferred_element_type=F32) * scale
            mine = s == pslot
            lo_t = jnp.where(mine, poff, CTX)
            ok = ((jc & 1) == 0) & (tc < len_s[s]) & ((tc < lo_t) | (tc >= lo_t + O))
            pre_lim = jnp.where(mine, O, 0)
            sc.append(jnp.where(ok, a, neg))
            se.append(jnp.where(fresh_ok | (lane_e < pre_lim), b, neg))
            xs.append(x)
            vs.append(ev)
        outs = []
        for s in range(S):
            top = jnp.maximum(jnp.max(sc[s], axis=1, keepdims=True), jnp.max(se[s], axis=1, keepdims=True))
            pa, pb = jnp.exp(sc[s] - top), jnp.exp(se[s] - top)
            inv = 1.0 / (jnp.sum(pa, axis=1, keepdims=True) + jnp.sum(pb, axis=1, keepdims=True))
            wa = pltpu.roll(pa * inv, 1, 1).astype(BF16)
            wb = (pb * inv).astype(BF16)
            outs.append(jnp.dot(wa, xs[s], preferred_element_type=F32)
                        + jnp.dot(wb, vs[s], preferred_element_type=F32))
        turned = []
        for d in range(DRAFT):
            rows = jnp.concatenate([o[d * GS:(d + 1) * GS] for o in outs], 0).astype(BF16)
            turned.append(jnp.dot(swap, rows, preferred_element_type=F32))
        for g in range(GS):
            gath[k, me, :, g * HD:(g + 1) * HD] = jnp.concatenate(
                [turned[0][g * S:(g + 1) * S], turned[1][g * S:(g + 1) * S]], 0).astype(BF16)
        for g in range(half):
            gath[k, me, :, gw + g * HD:gw + (g + 1) * HD] = jnp.concatenate(
                [turned[2][g * S:(g + 1) * S], turned[2][(g + half) * S:(g + half + 1) * S]], 0).astype(BF16)

    def g_copy(k, block, way):
        dev = [{"pool": z + 1}, {"pool": z - 1}, {"rep": 1 - core}][way]
        ref = gath.at[k, block]
        return pltpu.make_async_remote_copy(ref, ref, g_send.at[k, block, way], g_recv.at[k, block], dev, MESH)

    sends = []

    def g_start(k, cond, block, way):
        sends.append((k, cond, block, way))

        @pl.when(cond)
        def _():
            g_copy(k, block, way).start()

    always = z >= 0

    def hop(k, h):
        if h == 0:
            g_start(k, z < PL - 1, me, 0)
            g_start(k, z > 0, me, 1)
            g_start(k, always, me, 2)
            return
        for way, zz in ((0, z - h), (1, z + h)):
            there = (zz >= 0) & (zz < PL)
            block = jnp.clip(zz, 0, PL - 1) * R + core

            @pl.when(there)
            def _():
                wait_arrival(gath.at[k, block], g_recv.at[k, block])

            g_start(k, there & ((z < PL - 1) if way == 0 else (z > 0)), block, way)
            g_start(k, there, block, 2)

    def other_core(k):
        for zz in range(PL):
            block = zz * R + 1 - core
            wait_arrival(gath.at[k, block], g_recv.at[k, block])

    def picked(k, mats):
        g = gath[k].reshape(O * 2 * S, gw + gw // 2)
        a = jnp.dot(mats[0], g[:, :gw], preferred_element_type=F32)
        b = jnp.dot(mats[1], g[:, gw:], preferred_element_type=F32)
        c2 = jnp.dot(mats[2], g[:, gw:], preferred_element_type=F32)
        return (a + jnp.concatenate([b, c2], 1)).astype(BF16)

    def y_copy(n, i):
        p = lax.rem(me_t + i, T)
        return pltpu.make_async_remote_copy(
            ysend.at[n, p], yrecv.at[n, me_t], y_send.at[n, p], y_recv.at[n, me_t], {"tensor": p}, MESH)

    NCH = ysend.shape[0]
    cw = N // NCH

    def share(n):
        for t in range(T):
            ysend[n, t] = ytot[t * rows_t:(t + 1) * rows_t, n * cw:(n + 1) * cw].astype(BF16)
        for i in range(1, T):
            y_copy(n, i).start()

    def project(k):
        pltpu.make_async_copy(weight.at[pl.ds(k * gw, gw), :], wbuf.at[k], w_sem.at[k]).wait()
        if keep:
            rows = picked(k, [cmat[x] for x in range(3)])
            for n in range(NCH):
                cols = slice(n * cw, (n + 1) * cw)
                y = jnp.dot(rows, wbuf[k, :, cols], preferred_element_type=F32)
                ytot[:, cols] = y if k == 0 else ytot[:, cols] + y
                if k == K - 1:
                    share(n)
        else:
            def body(t, carry):
                rows = picked(k, out_onehots(meta_out[0, pl.ds(1 + t, 1), :]))
                at = pl.ds(pl.multiple_of(t * 128, 128), 128)
                y = jnp.dot(rows, wbuf[k], preferred_element_type=F32)
                ytot[at, :] = y if k == 0 else ytot[at, :] + y
                return carry

            lax.fori_loop(0, NT, body, 0)
            if k == K - 1:
                for n in range(NCH):
                    share(n)

    for step in range(K + PL):
        if step < K:
            k = step
            pltpu.make_async_copy(cache.at[:, :, :, pl.ds(k * HD, HD)], kvbuf.at[k], kv_sem.at[k]).wait()
            own_copies[1 + k].wait()
            for i in order:
                p, _ = peer(i)
                wait_arrival(recv.at[k, p], pk_recv.at[k, p])
            attend(k)
            hop(k, 0)
        for h in range(1, PL):
            if 0 <= step - h < K:
                hop(step - h, h)
        k = step - PL
        if 0 <= k < K:
            other_core(k)
            project(k)

    for n in range(NCH):
        cols = slice(n * cw, (n + 1) * cw)
        y = ytot[pl.ds(pl.multiple_of(me_t * rows_t, 32), rows_t), cols]
        for i in range(1, T):
            p = lax.rem(me_t + i, T)
            wait_arrival(yrecv.at[n, p], y_recv.at[n, p])
            y = y + yrecv[n, p].astype(F32)
        out[:, cols] = y.astype(BF16)

    if keep:
        for i in order:
            meta_copy(i).wait_send()
    for k in range(K):
        for i in order:
            pack_copy(k, i).wait_send()
    for k, cond, block, way in sends:
        @pl.when(cond)
        def _():
            g_copy(k, block, way).wait_send()
    for n in range(NCH):
        for i in range(1, T):
            y_copy(n, i).wait_send()


def on_device(request_slot, lengths, prefill_slot, prefill_offset, queries, new_kv, kv_cache,
              prefill_kv, out_weight):
    PLn, R, T = lax.axis_size("pool"), lax.axis_size("rep"), lax.axis_size("tensor")
    O = PLn * R
    S = lengths.shape[0]
    CTX = kv_cache.shape[1]
    K = kv_cache.shape[3] // HD
    GS = queries.shape[2] // kv_cache.shape[3]
    N = out_weight.shape[1]
    rows = O * S * DRAFT
    NT = up(rows, 128) // 128
    gw = GS * HD
    src = jnp.concatenate([
        queries.reshape(S, DRAFT, K, GS, HD).transpose(1, 0, 3, 2, 4).reshape(-1, K * HD),
        new_kv.transpose(1, 0, 2, 3).reshape(-1, K * HD),
        prefill_kv.reshape(-1, K * HD),
    ], 0)
    PR = max(16, O)
    MR = up(1 + NT, 8)
    perm_rows = S * DRAFT * GS + 2 * (S * 16 + PR)
    keep = NT <= 2
    NCH = 4
    dims = (S, O, R, T, K, CTX, GS, N, NT)
    scratch = [
        pltpu.VMEM((K, S, CTX, 2, HD), BF16),
        pltpu.VMEM((K, gw, N), BF16),
        pltpu.VMEM((K, O, PACK, HD), BF16),
        pltpu.VMEM((K, O, PACK, HD), BF16),
        pltpu.VMEM((O, MR, 128), jnp.int32),
        pltpu.VMEM((O, MR, 128), jnp.int32),
        pltpu.VMEM((perm_rows, O * PACK), BF16),
    ]
    if keep:
        scratch.append(pltpu.VMEM((3, NT * 128, O * 2 * S), BF16))
    scratch += [
        pltpu.VMEM((K, O, 2 * S, gw + gw // 2), BF16),
        pltpu.VMEM((NT * 128, N), F32),
        pltpu.VMEM((NCH, T, rows // T, N // NCH), BF16),
        pltpu.VMEM((NCH, T, rows // T, N // NCH), BF16),
    ]
    D = pltpu.SemaphoreType.DMA
    scratch += [D((K,)), D((K,)), D((K + 1,)), D((K, O)), D((K, O)), D((O,)), D((O,)),
                D((K, O, 3)), D((K, O)), D((NCH, T)), D((NCH, T))]
    if keep:
        body = functools.partial(kernel, dims)
    else:
        def body(*refs):
            return kernel(dims, *refs[:15], None, *refs[15:])
    smem = pl.BlockSpec(memory_space=pltpu.SMEM)
    vmem = pl.BlockSpec(memory_space=pltpu.VMEM)
    hbm = pl.BlockSpec(memory_space=pl.ANY)
    return pl.pallas_call(
        body,
        out_shape=jax.ShapeDtypeStruct((rows // T, N), BF16),
        in_specs=[smem] * 4 + [vmem, hbm, hbm],
        out_specs=vmem,
        scratch_shapes=scratch,
        compiler_params=pltpu.CompilerParams(
            collective_id=0, has_side_effects=True, vmem_limit_bytes=56 * 1024 * 1024),
        cost_estimate=pl.CostEstimate(flops=4 * 10 ** 9, bytes_accessed=12 * 10 ** 6, transcendentals=10 ** 6),
    )(request_slot, lengths, prefill_slot, prefill_offset, src, kv_cache, out_weight)


def solution(mesh):
    owner = ("groups", "pool", "rep")
    return jax.shard_map(
        on_device,
        mesh=mesh,
        in_specs=(
            P(owner), P(owner), P(owner), P(owner),
            P(owner, None, "tensor"),
            P(owner, None, None, "tensor"),
            P(owner, None, None, "tensor"),
            P("groups", ("pool", "rep"), None, "tensor"),
            P("tensor", ("pool", "rep")),
        ),
        out_specs=P(("groups", "tensor"), ("pool", "rep")),
        check_vma=False,
    )
```

time: 158 us -> 53.5 us (0.34)
  waiting for transfers between devices: 52.8 us -> 0 us
  Pallas kernels: 0 us -> 46.9 us
  local copies, waits for them, and re-layouts: 38.3 us -> 4.17 us
  starting transfers between devices: 19.4 us -> 0 us
  blocking collectives: 17.3 us -> 0 us
  between operations: 14.9 us -> 1.32 us
  matrix products: 12.2 us -> 0 us
  other arithmetic: 2.7 us -> 0.71 us
    pallas_call x0 -> x1, Pallas kernels: none -> 46.9 us  [on_device(): pl.pallas_call(body, out_shape=jax.ShapeDtypeStruct((rows // T, N), BF16)...]
    all_gather x1 -> x0, waiting for transfers between devices: 23.9 us -> none  [on_device(): lax.all_gather(own_rows, ('pool', 'rep'), axis=0, tiled=True)]
    all_to_all x4 -> x0, starting transfers between devices: 19.1 us -> none  [the longest x1 6.59 us: on_device(): lax.all_to_all(slot_pack, ('pool', 'rep'), split_axis=0, concat_axis=0, t...]
    slice x2 -> x0, local copies, waits for them, and re-layouts: 18.7 us -> none  [the longest x1 18.7 us: on_device(): value_rows = cache_now[:, :, 1].reshape(slot_count, -1, kv_heads, HEAD_DIM)]
    all_to_all x1 -> x0, blocking collectives: 17.3 us -> none  [on_device(): lax.all_to_all(outgoing, ('pool', 'rep'), split_axis=0, concat_axis=0, ti...]
    reduce_scatter x1 -> x0, waiting for transfers between devices: 17.1 us -> none  [on_device(): lax.psum_scatter(jnp.dot(gathered, out_weight, preferred_element_type=jnp...]
    dot_general x11 -> x0, matrix products: 12.2 us -> none  [the longest x1 6.55 us: on_device(): jnp.dot(gathered, out_weight, preferred_element_type=jnp.float32)]
    all_to_all x4 -> x0, waiting for transfers between devices: 11.8 us -> none  [the longest x1 6.23 us: on_device(): lax.all_to_all(pair_pack, ('pool', 'rep'), split_axis=0, concat_axis=0, t...]
  transfers between devices with their start and end apart: 6 -> 0, of which waited for: 4 -> 0; matrix products, arithmetic and copies ran while one was open for 19% -> 0% of each run, Pallas kernels for 0% -> 0%
where the time goes in v1:
time: 53.5 us; the launch traced here: 53.1 us
  Pallas kernels  46.9 us (88%)
  local copies, waits for them, and re-layouts  4.17 us (8%)
  between operations  1.32 us (2%)
  other arithmetic  0.71 us (1%)
    pallas_call x1, Pallas kernels, on_device(): pl.pallas_call(body, out_shape=jax.ShapeDtypeStruct((rows // T, N), BF16)...  46.9 us
    unnamed x1, local copies, waits for them, and re-layouts  1.62 us

profile of v1, /device:TPU:0, one launch (start us, length us, event | category | flops | bytes accessed | tf_op | source)
XLA Modules:
  0.0 53.1 jit_solution(15096233327811888870)
XLA Ops:
  0.0 1.0 %copy.10 = bf16[8,3,4,8,128]{4,3,2,0,1:T(8,128)(2,1)S(1)} copy(bf16[8,3,4,8,128]{4,0,3,2,1:T(8,128)(2,1)} %bitcast.6) | data formatting | bytes 393216 | tf_op jit(solution)/shard_map/reshape | solution.py:396
  1.0 0.8 %copy.11 = bf16[3,8,2,512]{3,2,1,0:T(2,128)(2,1)S(1)} copy(bf16[3,8,2,512]{3,2,0,1:T(2,128)(2,1)} %bitcast.7) | data formatting | bytes 98304 | tf_op jit(solution)/shard_map/transpose | solution.py:397
  1.8 0.7 %reshape.15 = bf16[16,512]{1,0:T(8,128)(2,1)S(1)} reshape(bf16[8,1,2,512]{3,2,1,0:T(2,128)(2,1)} %param.16) | data formatting | bytes 32768 | tf_op jit(solution)/shard_map/reshape | solution.py:398
  2.6 0.7 %pad_maximum_fusion.src = bf16[256,512]{1,0:T(8,128)(2,1)} fusion(bf16[16,512]{1,0:T(8,128)(2,1)S(1)} %reshape.15, bf16[48,512]{1,0:T(8,128)(2,1)S(1)} %reshape.14, bf16[192,512]{1,0:T(8,128)(2,1)S(1)} %bitcast.5), kind=kLoop, calls=%fused_computation | loop fusion | flops 786432 | bytes 524288 | tf_op jit(solution)/shard_map/concatenate | solution.py:395
  4.6 46.9 %shard_map.91 = bf16[96,1024]{1,0:T(8,128)(2,1)} custom-call(s32[8]{0:T(128)} %slot_s.1, s32[8]{0:T(128)} %len_s.1, s32[1]{0:T(128)S(6)} %copy.13.pslot_s, s32[1]{0:T(128)S(6)} %copy.14.poff_s, bf16[256,512]{1,0:T(8,128)(2,1)} %pad_maximum_fusion.src, bf16[8,192,2,512]{3,2,1,0:T(2,128)(2,1)} %cache.1, bf16[4096,1024]{1,0:T(8,128)(2,1)} %weight.1), custom_call_target="tpu_custom_call" | custom-call | flops 4000000000 | bytes 12000000 | tf_op jit(solution)/shard_map/pallas_call | solution.py:434
  51.5 1.6 %copy.15 = bf16[96,1024]{1,0:T(8,128)(2,1)} copy(bf16[96,1024]{1,0:T(8,128)(2,1)} %shard_map.91) | data formatting | bytes 393216
  (1 shorter events, 0.0 us)

commit v2 on v1

--- a/solution.py
+++ b/solution.py
@@ -47,9 +47,6 @@
     for k in range(K):
         pltpu.make_async_copy(
             cache.at[:, :, :, pl.ds(k * HD, HD)], kvbuf.at[k], kv_sem.at[k]).start()
-    for k in range(K):
-        pltpu.make_async_copy(
-            weight.at[pl.ds(k * gw, gw), :], wbuf.at[k], w_sem.at[k]).start()
 
     barrier = pltpu.get_barrier_semaphore()
     for i in range(1, O):
@@ -86,7 +83,10 @@
     pre = c - NQ - NF
     is_q = c < NQ
     is_f = (c >= NQ) & (pre < 0)
-    rcol = jnp.where(is_q, (c >> lg) & (S - 1), jnp.where(is_f, (f >> 1) & (S - 1), -1))
+    rf = jnp.zeros((1, NC), jnp.int32)
+    for r in range(1, S):
+        rf = rf + jnp.where(f >= r * 2 * DRAFT, 1, 0)
+    rcol = jnp.where(is_q, (c >> lg) & (S - 1), jnp.where(is_f, rf, -1))
     ocol = jnp.zeros((1, NC), jnp.int32) - 1
     for r in range(S):
         ocol = jnp.where(rcol == r, slots[r] >> ls, ocol)
@@ -96,7 +96,7 @@
     code = (ocol * CAP + rank) * KEYS
     ckey = jnp.where(
         is_q, code + (c >> (lg + ls)) * GS + (c & (GS - 1)),
-        jnp.where(is_f, code + 24 + (f >> (1 + ls)) * 2 + (f & 1),
+        jnp.where(is_f, code + 24 + f - rf * 2 * DRAFT,
                   (pre >> 1) * CAP * KEYS + 32 + (pre & 1)))
     OB = min(O, 8)
     jr = iota((OB * PACK, 1), 0)
@@ -139,6 +139,9 @@
     for k in range(K):
         for i in order:
             pack_copy(k, i).start()
+    for k in range(K):
+        pltpu.make_async_copy(
+            weight.at[pl.ds(k * gw, gw), :], wbuf.at[k], w_sem.at[k]).start()
 
     def wait_arrival(buf, sem):
         pltpu.make_async_copy(buf, buf, sem).wait()
@@ -190,11 +193,7 @@
     for o in range(1, O):
         total = total + meta_in[o]
     keep = cmat is not None
-    if keep:
-        for t in range(NT):
-            for x, m in enumerate(out_onehots(total[1 + t:2 + t])):
-                cmat[x, t * 128:(t + 1) * 128, :] = m
-    else:
+    if not keep:
         for i in order:
             meta_copy(i).wait_send()
         meta_out[0] = total
@@ -348,7 +347,11 @@
                 wait_arrival(recv.at[k, p], pk_recv.at[k, p])
             attend(k)
             hop(k, 0)
-        for h in range(1, PL):
+            if keep and k == 0:
+                for t in range(NT):
+                    for x, m in enumerate(out_onehots(total[1 + t:2 + t])):
+                        cmat[x, t * 128:(t + 1) * 128, :] = m
+        for h in range(PL - 1, 0, -1):
             if 0 <= step - h < K:
                 hop(step - h, h)
         k = step - PL
@@ -392,16 +395,15 @@
     rows = O * S * DRAFT
     NT = up(rows, 128) // 128
     gw = GS * HD
-    src = jnp.concatenate([
-        queries.reshape(S, DRAFT, K, GS, HD).transpose(1, 0, 3, 2, 4).reshape(-1, K * HD),
-        new_kv.transpose(1, 0, 2, 3).reshape(-1, K * HD),
-        prefill_kv.reshape(-1, K * HD),
-    ], 0)
+    src_q = queries.reshape(S, DRAFT, K, GS, HD).transpose(1, 0, 3, 2, 4).reshape(-1, K * HD)
+    src_f = new_kv.reshape(-1, K * HD)
+    src_p = prefill_kv.reshape(-1, K * HD)
+    src = jnp.concatenate([src_q, src_f, src_p], 0)
     PR = max(16, O)
     MR = up(1 + NT, 8)
     perm_rows = S * DRAFT * GS + 2 * (S * 16 + PR)
     keep = NT <= 2
-    NCH = 4
+    NCH = 2
     dims = (S, O, R, T, K, CTX, GS, N, NT)
     scratch = [
         pltpu.VMEM((K, S, CTX, 2, HD), BF16),

time: 53.5 us -> 54 us (level)
  Pallas kernels: 46.9 us -> 47.6 us
    transpose x1 -> x0, local copies, waits for them, and re-layouts: 0.84 us -> none  [on_device(): new_kv.transpose(1, 0, 2, 3).reshape(-1, K * HD)]
    reshape x2, local copies, waits for them, and re-layouts: 0.76 us -> 1.56 us  [the longest x1 0.83 us: on_device(): src_f = new_kv.reshape(-1, K * HD)]
    pallas_call x1, Pallas kernels: 46.9 us -> 47.6 us  [on_device(): pl.pallas_call(body, out_shape=jax.ShapeDtypeStruct((rows // T, N), BF16)...]
where the time goes in v2:
time: 54 us; the launch traced here: 53.7 us
  Pallas kernels  47.6 us (88%)
  local copies, waits for them, and re-layouts  4.13 us (8%)
  between operations  1.32 us (2%)
  other arithmetic  0.71 us (1%)
    pallas_call x1, Pallas kernels, on_device(): pl.pallas_call(body, out_shape=jax.ShapeDtypeStruct((rows // T, N), BF16)...  47.6 us
    unnamed x1, local copies, waits for them, and re-layouts  1.62 us

profile of v2, /device:TPU:0, one launch (start us, length us, event | category | flops | bytes accessed | tf_op | source)
XLA Modules:
  0.0 53.7 jit_solution(7118583007632456181)
XLA Ops:
  0.0 1.0 %copy.10 = bf16[8,3,4,8,128]{4,3,2,0,1:T(8,128)(2,1)S(1)} copy(bf16[8,3,4,8,128]{4,0,3,2,1:T(8,128)(2,1)} %bitcast.5) | data formatting | bytes 393216 | tf_op jit(solution)/shard_map/reshape | solution.py:398
  1.0 0.8 %reshape.14 = bf16[48,512]{1,0:T(8,128)(2,1)S(1)} reshape(bf16[8,3,2,512]{3,2,1,0:T(2,128)(2,1)} %param.14) | data formatting | bytes 98304 | tf_op jit(solution)/shard_map/reshape | solution.py:399
  1.8 0.7 %reshape.15 = bf16[16,512]{1,0:T(8,128)(2,1)S(1)} reshape(bf16[8,1,2,512]{3,2,1,0:T(2,128)(2,1)} %param.16) | data formatting | bytes 32768 | tf_op jit(solution)/shard_map/reshape | solution.py:400
  2.5 0.7 %pad_maximum_fusion.src = bf16[256,512]{1,0:T(8,128)(2,1)} fusion(bf16[16,512]{1,0:T(8,128)(2,1)S(1)} %reshape.15, bf16[48,512]{1,0:T(8,128)(2,1)S(1)} %reshape.14, bf16[192,512]{1,0:T(8,128)(2,1)S(1)} %bitcast.4), kind=kLoop, calls=%fused_computation | loop fusion | flops 786432 | bytes 524288 | tf_op jit(solution)/shard_map/concatenate | solution.py:401
  4.5 47.6 %shard_map.91 = bf16[96,1024]{1,0:T(8,128)(2,1)} custom-call(s32[8]{0:T(128)} %slot_s.1, s32[8]{0:T(128)} %len_s.1, s32[1]{0:T(128)S(6)} %copy.12.pslot_s, s32[1]{0:T(128)S(6)} %copy.13.poff_s, bf16[256,512]{1,0:T(8,128)(2,1)} %pad_maximum_fusion.src, bf16[8,192,2,512]{3,2,1,0:T(2,128)(2,1)} %cache.1, bf16[4096,1024]{1,0:T(8,128)(2,1)} %weight.1), custom_call_target="tpu_custom_call" | custom-call | flops 4000000000 | bytes 12000000 | tf_op jit(solution)/shard_map/pallas_call | solution.py:436
  52.1 1.6 %copy.14 = bf16[96,1024]{1,0:T(8,128)(2,1)} copy(bf16[96,1024]{1,0:T(8,128)(2,1)} %shard_map.91) | data formatting | bytes 393216
